TPU v7x, 32 devices: a whole 2x2x4 slice. The times are simulated.
32 devices in a mesh: rep: 2 (over x), shard: 16 (over z, y, core).
Axes of the slice: x: 2, y: 2, z: 4, core: 2. Of those that a mesh axis runs over, the one named last changes fastest.
Arguments:
- tokens: bfloat16 [4096, 768], P(('rep', 'shard')), may hold values from -6 to 6
- cotangent: bfloat16 [4096, 768], P(('rep', 'shard')), may hold values from -6 to 6
- lengths: int32 [32, 3], P(('rep', 'shard')), may hold values from 1 to 96, 128 in all within a row
- routes: int32 [4096, 1], P(('rep', 'shard')), may hold values from 0 to 1; in each aligned block of 128 rows (0 to 127, 128 to 255, ...) at most 80 rows name the same one
- bucket_ids: int32 [255], replicated, may hold values from 0 to 31
- attn_in: bfloat16 [3, 768, 768], P(None, 'shard'), may hold values from -0.21875 to 0.21875
- attn_out: bfloat16 [768, 768], P('shard'), may hold values from -0.875 to 0.875
- gains: bfloat16 [2, 768], P(None, 'shard'), may hold values from 0.25 to 1.75
- router: bfloat16 [768, 2], P('shard'), may hold values from -0.109375 to 0.109375
- rel_table: bfloat16 [32, 12], P('shard'), may hold values from -4 to 4
- expert_in: bfloat16 [2, 768, 3072], P(None, 'shard'), may hold values from -0.21875 to 0.21875
- expert_out: bfloat16 [2, 3072, 768], P(None, 'shard'), may hold values from -0.21875 to 0.21875
Outputs:
- layer_out: bfloat16 [4096, 768], P(('rep', 'shard'))
- input_grad: float32 [4096, 768], P(('rep', 'shard'))
- grad_attn_in: float32 [3, 768, 768], P(None, 'shard')
- grad_attn_out: float32 [768, 768], P('shard')
- grad_gains: float32 [2, 768], P(None, 'shard')
- grad_router: float32 [768, 2], P('shard')
- grad_rel_table: float32 [32, 12], P('shard')
- grad_expert_in: float32 [2, 768, 3072], P(None, 'shard')
- grad_expert_out: float32 [2, 3072, 768], P(None, 'shard')
Inputs may be any that keep to these rules, and one draw needn't show every extreme that they name: Row b holds the lengths of the 3 sequences of device block b; they sum to 128, and some block has one of exactly 96. `routes`: within the 128 rows of one device no expert is named more than 80 times, and in every draw some device names some expert exactly 80 times.
All inputs are finite; a program needn't handle non-finite values.
Results may differ from a plain program's by a relative error of at most 0.012.
Values may be sent and summed in bfloat16 or wider, within the bound.
A program may use at most 192 MiB of HBM per device.

v0:
```python
import jax
import jax.numpy as jnp
from jax import lax
from jax.sharding import PartitionSpec as P

BUCKETS = 32
CAP = 80
epsilon = 1e-06


def rms_norm(values, gain):
    return values * lax.rsqrt(jnp.mean(values * values, axis=-1, keepdims=True) + epsilon) * gain


def gelu_tanh(values):
    return jax.nn.gelu(values, approximate=True)


def offsets_to_pairs(per_offset, length):
    heads = per_offset.shape[0]
    reverse = per_offset[:, ::-1]
    repeated = jnp.broadcast_to(reverse[:, None, :], (heads, length, 2 * length - 1))
    repeated = repeated.reshape(heads, length * (2 * length - 1))
    repeated = jnp.pad(repeated, ((0, 0), (0, length)))
    skewed = repeated.reshape(heads, length, 2 * length)[:, :, :length]
    return skewed[:, :, ::-1]


def pairs_to_offsets(grid, length):
    heads = grid.shape[0]
    flipped = grid[:, :, ::-1]
    padded = jnp.pad(flipped, ((0, 0), (0, 0), (0, length)))
    flat = padded.reshape(heads, 2 * length * length)[:, : length * (2 * length - 1)]
    skewed = flat.reshape(heads, length, 2 * length - 1)
    return jnp.sum(skewed, axis=1)[:, ::-1]


def shards(
    tokens,
    cotangent,
    lengths,
    routes,
    bucket_ids,
    attn_in,
    attn_out,
    gains,
    router,
    rel_table,
    expert_in,
    expert_out,
):
    highest = lax.Precision.HIGHEST
    length = tokens.shape[0]
    width = tokens.shape[1]
    heads = rel_table.shape[1]
    head_size = width // heads
    experts = expert_in.shape[0]
    capacity = CAP
    bucket_count = BUCKETS
    full_in, full_out, full_gains, full_router, full_table = (
        lax.all_gather(attn_in, "shard", axis=1, tiled=True),
        lax.all_gather(attn_out, "shard", axis=0, tiled=True),
        lax.all_gather(gains, "shard", axis=1, tiled=True),
        lax.all_gather(router, "shard", axis=0, tiled=True),
        lax.all_gather(rel_table, "shard", axis=0, tiled=True),
    )
    inputs = tokens.astype(jnp.float32)
    gain_attn = full_gains[0].astype(jnp.float32)
    gain_ffn = full_gains[1].astype(jnp.float32)
    normed = rms_norm(inputs, gain_attn).astype(jnp.bfloat16)
    projected = jnp.einsum(
        "td,kde->kte", normed, full_in, preferred_element_type=jnp.float32
    ).astype(jnp.bfloat16)
    query = projected[0].reshape(length, heads, head_size)
    keys = projected[1].reshape(length, heads, head_size)
    values = projected[2].reshape(length, heads, head_size)
    places = jnp.arange(length, dtype=jnp.int32)
    offset_onehot = (
        bucket_ids[:, None] == jnp.arange(bucket_count, dtype=jnp.int32)[None, :]
    ).astype(jnp.float32)
    offset_bias = jnp.einsum(
        "ob,bh->ho", offset_onehot, full_table.astype(jnp.float32), precision=highest
    )
    bias = offsets_to_pairs(offset_bias, length)
    ends = jnp.cumsum(lengths[0])
    segment = jnp.sum((places[:, None] >= ends[None, :]).astype(jnp.int32), axis=1)
    allowed = segment[:, None] == segment[None, :]

    def masked_scores():
        raw = jnp.einsum("qhc,khc->hqk", query, keys, preferred_element_type=jnp.float32) * 0.125
        return jnp.where(allowed[None], raw + bias, -1e30)

    scores = masked_scores()
    peak = jnp.max(scores, axis=-1, keepdims=True)
    expo = jnp.exp(scores - peak)
    totals = jnp.sum(expo, axis=-1, keepdims=True)
    logsum = peak + jnp.log(totals)
    probs_low = (expo / totals).astype(jnp.bfloat16)
    context = jnp.einsum("hqk,khc->qhc", probs_low, values, preferred_element_type=jnp.float32)
    context = context.astype(jnp.bfloat16).reshape(length, width)
    hidden = inputs + jnp.dot(context, full_out, preferred_element_type=jnp.float32)
    normed_ffn = rms_norm(hidden, gain_ffn).astype(jnp.bfloat16)
    logits = jnp.dot(normed_ffn, full_router, preferred_element_type=jnp.float32)
    gate_probs = jax.nn.softmax(logits, axis=-1)
    chosen = routes[:, 0]
    picked = chosen[:, None] == jnp.arange(experts, dtype=jnp.int32)[None, :]
    gate = jnp.sum(jnp.where(picked, gate_probs, 0.0), axis=1)
    ranks = jnp.cumsum(picked.astype(jnp.int32), axis=0) - 1
    slot = chosen * capacity + jnp.sum(jnp.where(picked, ranks, 0), axis=1)
    dispatch = (jnp.arange(experts * capacity, dtype=jnp.int32)[:, None] == slot[None, :]).astype(
        jnp.bfloat16
    )
    buffers = jnp.dot(dispatch, normed_ffn, preferred_element_type=jnp.float32).astype(jnp.bfloat16)
    buffers = buffers.reshape(experts, capacity, width)
    before_list = []
    active_list = []
    returned_list = []
    for expert in range(experts):
        batch = buffers[expert]
        whole_in = lax.all_gather(expert_in[expert], "shard", axis=0, tiled=True)
        before = jnp.dot(batch, whole_in, preferred_element_type=jnp.float32)
        active = gelu_tanh(before).astype(jnp.bfloat16)
        whole_out = lax.all_gather(expert_out[expert], "shard", axis=0, tiled=True)
        returned = jnp.dot(active, whole_out, preferred_element_type=jnp.float32)
        before_list.append(before)
        active_list.append(active)
        returned_list.append(returned)
    returned_all = jnp.concatenate(returned_list, axis=0)
    gathered = jnp.take(returned_all, slot, axis=0)
    layer_out = (hidden + gate[:, None] * gathered).astype(jnp.bfloat16)
    upstream = cotangent.astype(jnp.float32)
    gate_grad = jnp.sum(upstream * gathered, axis=1)
    scaled = (gate[:, None] * upstream).astype(jnp.bfloat16)
    returned_grad = jnp.dot(dispatch, scaled, preferred_element_type=jnp.float32).astype(
        jnp.bfloat16
    )
    returned_grad = returned_grad.reshape(experts, capacity, width)
    batch_grads = []
    inner_shards = []
    outer_shards = []
    for expert in range(experts):
        batch = buffers[expert]
        active = active_list[expert]
        out_grad = returned_grad[expert]
        out_matrix = lax.all_gather(expert_out[expert], "shard", axis=0, tiled=True)
        active_grad = jnp.einsum(
            "cd,fd->cf", out_grad, out_matrix, preferred_element_type=jnp.float32
        )
        before_grad = jax.vjp(gelu_tanh, before_list[expert])[1](active_grad)[0].astype(
            jnp.bfloat16
        )
        in_matrix = lax.all_gather(expert_in[expert], "shard", axis=0, tiled=True)
        batch_grad = jnp.einsum(
            "cf,df->cd", before_grad, in_matrix, preferred_element_type=jnp.float32
        )
        batch_grads.append(batch_grad)
        inner_shard = lax.psum_scatter(
            jnp.einsum("cd,cf->df", batch, before_grad, preferred_element_type=jnp.float32),
            "shard",
            scatter_dimension=0,
            tiled=True,
        )
        outer_shard = lax.psum_scatter(
            jnp.einsum("cf,cd->fd", active, out_grad, preferred_element_type=jnp.float32),
            "shard",
            scatter_dimension=0,
            tiled=True,
        )
        inner_shards.append(inner_shard)
        outer_shards.append(outer_shard)
    batch_all = jnp.concatenate(batch_grads, axis=0)
    ffn_normed_grad = jnp.take(batch_all, slot, axis=0)
    prob_grad = jnp.where(picked, gate_grad[:, None], 0.0)
    logit_grad = gate_probs * (prob_grad - jnp.sum(gate_probs * prob_grad, axis=1, keepdims=True))
    normed_wide = normed_ffn.astype(jnp.float32)
    router_grad = jnp.einsum("td,te->de", normed_wide, logit_grad, precision=highest)
    ffn_normed_grad = ffn_normed_grad + jnp.einsum(
        "te,de->td", logit_grad, full_router.astype(jnp.float32), precision=highest
    )
    norm_pull = jax.vjp(rms_norm, hidden, gain_ffn)[1]
    hidden_from_norm, gain_ffn_grad = norm_pull(ffn_normed_grad)
    hidden_grad = upstream + hidden_from_norm
    attn_grad = hidden_grad.astype(jnp.bfloat16)
    attn_out_grad = jnp.einsum("td,te->de", context, attn_grad, preferred_element_type=jnp.float32)
    context_grad = jnp.einsum("te,de->td", attn_grad, full_out, preferred_element_type=jnp.float32)
    context_grad = context_grad.astype(jnp.bfloat16).reshape(length, heads, head_size)
    probs = jnp.exp(masked_scores() - logsum)
    probs_back = probs.astype(jnp.bfloat16)
    prob_grad_attn = jnp.einsum(
        "qhc,khc->hqk", context_grad, values, preferred_element_type=jnp.float32
    )
    value_grad = jnp.einsum(
        "hqk,qhc->khc", probs_back, context_grad, preferred_element_type=jnp.float32
    )
    score_grad = probs * (prob_grad_attn - jnp.sum(probs * prob_grad_attn, axis=-1, keepdims=True))
    offset_grad = pairs_to_offsets(score_grad, length)
    table_grad = jnp.einsum("ho,ob->bh", offset_grad, offset_onehot, precision=highest)
    score_low = score_grad.astype(jnp.bfloat16)
    query_grad = (
        jnp.einsum("hqk,khc->qhc", score_low, keys, preferred_element_type=jnp.float32) * 0.125
    )
    key_grad = (
        jnp.einsum("hqk,qhc->khc", score_low, query, preferred_element_type=jnp.float32) * 0.125
    )
    projected_grad = jnp.stack(
        [
            query_grad.reshape(length, width),
            key_grad.reshape(length, width),
            value_grad.reshape(length, width),
        ]
    ).astype(jnp.bfloat16)
    attn_in_grad = jnp.einsum(
        "td,kte->kde", normed, projected_grad, preferred_element_type=jnp.float32
    )
    normed_grad = jnp.einsum(
        "kte,kde->td", projected_grad, full_in, preferred_element_type=jnp.float32
    )
    input_pull = jax.vjp(rms_norm, inputs, gain_attn)[1]
    input_from_norm, gain_attn_grad = input_pull(normed_grad)
    input_grad = hidden_grad + input_from_norm
    gains_grad = jnp.stack([gain_attn_grad, gain_ffn_grad])
    in_shard, out_shard, gains_shard, router_shard, table_shard = (
        lax.psum_scatter(attn_in_grad, "shard", scatter_dimension=1, tiled=True),
        lax.psum_scatter(attn_out_grad, "shard", scatter_dimension=0, tiled=True),
        lax.psum_scatter(gains_grad, "shard", scatter_dimension=1, tiled=True),
        lax.psum_scatter(router_grad, "shard", scatter_dimension=0, tiled=True),
        lax.psum_scatter(table_grad, "shard", scatter_dimension=0, tiled=True),
    )
    expert_in_grad = jnp.stack(inner_shards)
    expert_out_grad = jnp.stack(outer_shards)
    in_shard, out_shard, gains_shard, router_shard, table_shard, expert_in_grad, expert_out_grad = (
        lax.psum(
            (
                in_shard,
                out_shard,
                gains_shard,
                router_shard,
                table_shard,
                expert_in_grad,
                expert_out_grad,
            ),
            "rep",
        )
    )
    return (
        layer_out,
        input_grad,
        in_shard,
        out_shard,
        gains_shard,
        router_shard,
        table_shard,
        expert_in_grad,
        expert_out_grad,
    )


def solution(mesh):
    placed = (
        P(("rep", "shard"), None),
        P(("rep", "shard"), None),
        P(("rep", "shard"), None),
        P(("rep", "shard"), None),
        P(),
        P(None, "shard", None),
        P("shard", None),
        P(None, "shard"),
        P("shard", None),
        P("shard", None),
        P(None, "shard", None),
        P(None, "shard", None),
    )
    return jax.shard_map(
        shards,
        mesh=mesh,
        in_specs=placed,
        out_specs=(
            P(("rep", "shard"), None),
            P(("rep", "shard"), None),
            P(None, "shard", None),
            P("shard", None),
            P(None, "shard"),
            P("shard", None),
            P("shard", None),
            P(None, "shard", None),
            P(None, "shard", None),
        ),
        check_vma=False,
    )
```

profile of v0, /device:TPU:0, one launch (start us, length us, event | category | flops | bytes accessed | tf_op | source)
XLA Modules:
  0.0 1300.3 jit_solution(768440275594427823)
XLA Ops:
  8.7 1.9 fusion.96
  11.3 1.9 fusion.97
  13.8 23.2 %all-gather.4 = bf16[16,48,2]{1,2,0:T(2,128)(2,1)S(1)} all-gather(bf16[1,48,2]{1,2,0:T(2,128)(2,1)} %bitcast.144), channel_id=1, replica_groups=mesh['rep'=2,'shard'=16] {'shard'}, dimensions={0}, use_global_device_ids=true | all-gather | bytes 3264 | tf_op jit(solution)/shard_map/all_gather | solution.py:63
  37.1 17.5 %all-gather.6 = bf16[16,48,2]{1,2,0:T(2,128)(2,1)S(1)} all-gather(bf16[1,48,2]{1,2,0:T(2,128)(2,1)} %bitcast.145), channel_id=1, replica_groups=mesh['rep'=2,'shard'=16] {'shard'}, dimensions={0}, use_global_device_ids=true | all-gather | bytes 3264 | tf_op jit(solution)/shard_map/all_gather | solution.py:64
  54.7 18.9 %all-gather.5 = bf16[16,2,12]{2,1,0:T(2,128)(2,1)S(1)} all-gather(bf16[1,2,12]{2,1,0:T(2,128)(2,1)} %bitcast.146), channel_id=1, replica_groups=mesh['rep'=2,'shard'=16] {'shard'}, dimensions={0}, use_global_device_ids=true | all-gather | bytes 816 | tf_op jit(solution)/shard_map/all_gather | solution.py:65
  77.9 2.5 reshape.172
  82.5 2.7 fusion.18
  86.5 13.4 %all-gather.16.cloned.1.call-done = bf16[768,768]{1,0:T(8,128)(2,1)} async-done(((bf16[48,768]{1,0:T(8,128)(2,1)}), bf16[768,768]{1,0:T(8,128)(2,1)}) %all-gather.16.cloned.1.call-update) | async-done | bytes 1179664 | tf_op jit(solution)/shard_map/all_gather | solution.py:62
  99.9 1.7 multiply_reduce_fusion.3
  103.0 51.6 %all-gather.22.cloned.1.call-done = bf16[1,768,3072]{2,1,0:T(8,128)(2,1)} async-done(((bf16[1,48,3072]{2,1,0:T(8,128)(2,1)}), bf16[1,768,3072]{2,1,0:T(8,128)(2,1)}) %all-gather.22.cloned.1.call-update) | async-done | bytes 4718608 | tf_op jit(solution)/shard_map/all_gather | solution.py:120
  154.6 3.3 fusion.6
  157.9 51.4 %all-gather.18.cloned.1.call-done = bf16[1,768,3072]{2,1,0:T(8,128)(2,1)} async-done(((bf16[1,48,3072]{2,1,0:T(8,128)(2,1)}), bf16[1,768,3072]{2,1,0:T(8,128)(2,1)}) %all-gather.18.cloned.1.call-update) | async-done | bytes 4718608 | tf_op jit(solution)/shard_map/all_gather | solution.py:120
  209.3 3.3 fusion.14
  212.6 51.4 %all-gather.24.cloned.1.call-done = bf16[1,3072,768]{2,1,0:T(8,128)(2,1)} async-done(((bf16[1,192,768]{2,1,0:T(8,128)(2,1)}), bf16[1,3072,768]{2,1,0:T(8,128)(2,1)}) %all-gather.24.cloned.1.call-update) | async-done | bytes 4718608 | tf_op jit(solution)/shard_map/all_gather | solution.py:123
  264.0 4.0 fusion.2
  268.0 50.7 %all-gather.20.cloned.1.call-done = bf16[1,3072,768]{2,1,0:T(8,128)(2,1)} async-done(((bf16[1,192,768]{2,1,0:T(8,128)(2,1)}), bf16[1,3072,768]{2,1,0:T(8,128)(2,1)}) %all-gather.20.cloned.1.call-update) | async-done | bytes 4718608 | tf_op jit(solution)/shard_map/all_gather | solution.py:123
  318.7 3.4 fusion.10
  326.5 4.1 fusion.34
  337.1 1.6 multiply_reduce_fusion.1
  338.8 2.1 convert_add_fusion
  340.9 2.5 convolution_convert_fusion.4
  343.4 1.7 copy.88
  345.1 2.0 convolution_convert_fusion.3
  352.9 4.1 convolution_bitcast_fusion
  357.0 11.0 copy.96
  369.2 5.7 fusion.67
  375.9 5.1 fusion.64
  381.9 5.1 fusion.61
  387.1 5.0 fusion.58
  393.0 1.8 fusion.72
  396.2 3.5 fusion.44
  402.0 149.6 %all-reduce.9.cloned.1.call-done = f32[3,768,768]{2,0,1:T(4,128)} async-done(((f32[3,768,768]{2,0,1:T(4,128)}), f32[3,768,768]{2,0,1:T(4,128)}) %all-reduce.9.cloned.1.call-update) | async-done | bytes 7077904
  551.6 2.0 constant_dynamic-slice_fusion.1
  553.6 114.1 %reduce-scatter.14.cloned.1.call-done = f32[48,3072]{1,0:T(8,128)} async-done(((f32[768,3072]{1,0:T(8,128)}), f32[48,3072]{1,0:T(8,128)}) %reduce-scatter.14.cloned.1.call-update) | async-done | bytes 589840 | tf_op jit(solution)/shard_map/reduce_scatter | solution.py:157
  667.6 115.2 %reduce-scatter.16.cloned.1.call-done = f32[48,3072]{1,0:T(8,128)} async-done(((f32[768,3072]{1,0:T(8,128)}), f32[48,3072]{1,0:T(8,128)}) %reduce-scatter.16.cloned.1.call-update) | async-done | bytes 589840 | tf_op jit(solution)/shard_map/reduce_scatter | solution.py:157
  782.9 2.3 pad_maximum_fusion
  785.2 113.3 %reduce-scatter.18.cloned.1.call-done = f32[192,768]{1,0:T(8,128)} async-done(((f32[3072,768]{1,0:T(8,128)}), f32[192,768]{1,0:T(8,128)}) %reduce-scatter.18.cloned.1.call-update) | async-done | bytes 589840 | tf_op jit(solution)/shard_map/reduce_scatter | solution.py:163
  898.6 115.2 %reduce-scatter.20.cloned.1.call-done = f32[192,768]{1,0:T(8,128)} async-done(((f32[3072,768]{1,0:T(8,128)}), f32[192,768]{1,0:T(8,128)}) %reduce-scatter.20.cloned.1.call-update) | async-done | bytes 589840 | tf_op jit(solution)/shard_map/reduce_scatter | solution.py:163
  1013.8 2.3 pad_maximum_fusion.1
  1016.1 64.5 %reduce-scatter.12.cloned.1.call-done = f32[48,768]{1,0:T(8,128)} async-done(((f32[768,768]{1,0:T(8,128)}), f32[48,768]{1,0:T(8,128)}) %reduce-scatter.12.cloned.1.call-update) | async-done | bytes 147472 | tf_op jit(solution)/shard_map/reduce_scatter | solution.py:224
  1083.9 3.4 reshape.179
  1089.3 57.6 %all-reduce.3 = f32[32,12]{1,0:T(8,128)S(1)} all-reduce(f32[32,12]{1,0:T(8,128)S(1)} %fusion.75), channel_id=10, replica_groups=mesh['rep'=2,'shard'=16] {'shard'}, use_global_device_ids=true, to_apply=%region_27.29.clone | all-reduce | flops 384 | bytes 3072
  1148.7 49.0 %reduce-scatter.24.cloned.1.call-done = f32[48,2]{1,0:T(8,128)} async-done(((f32[768,2]{1,0:T(8,128)}), f32[48,2]{1,0:T(8,128)}) %reduce-scatter.24.cloned.1.call-update) | async-done | bytes 400
  1198.5 5.5 all-reduce.4
  1204.0 81.5 %all-reduce.11.cloned.1.call-done = (f32[3,48,768]{2,0,1:T(4,128)}, f32[48,768]{1,0:T(8,128)}, f32[2,48,3072]{2,1,0:T(8,128)}, f32[2,192,768]{2,1,0:T(8,128)}) async-done(((f32[3,48,768]{2,0,1:T(4,128)}, f32[48,768]{1,0:T(8,128)}, f32[2,48,3072]{2,1,0:T(8,128)}, f32[2,192,768]{2,1,0:T(8,128)}), (f32[3,48,768]{2,0,1:T(4,128)}, f32[48,768]{1,0:T(8,128)}, f32[2,48,3072]{2,1,0:T(8,128)}, ...) | async-done | bytes 2949136 | tf_op jit(solution)/shard_map/psum | solution.py:232
  1285.5 1.9 copy.98
  1289.0 2.4 copy.118
  1291.4 2.4 copy.119
  (181 shorter events, 43.8 us)
Async XLA Ops:
  7.2 75.3 %all-gather.14.cloned.1.call-start = ((), (), s32[]{:S(2)}) async-start(), calls=%async_computation.7 | async-start | bytes 3760128 | tf_op jit(solution)/shard_map/all_gather | solution.py:61
  7.9 92.0 %all-gather.16.cloned.1.call-start = ((), (), s32[]{:S(2)}) async-start(), calls=%async_computation.8 | async-start | bytes 1253376 | tf_op jit(solution)/shard_map/all_gather | solution.py:62
  8.7 146.0 %all-gather.22.cloned.1.call-start = ((), (), s32[]{:S(2)}) async-start(), calls=%async_computation.16 | async-start | bytes 5013504 | tf_op jit(solution)/shard_map/all_gather | solution.py:120
  10.6 198.7 %all-gather.18.cloned.1.call-start = ((), (), s32[]{:S(2)}) async-start(), calls=%async_computation.14 | async-start | bytes 5013504 | tf_op jit(solution)/shard_map/all_gather | solution.py:120
  11.2 252.8 %all-gather.24.cloned.1.call-start = ((), (), s32[]{:S(2)}) async-start(), calls=%async_computation.17 | async-start | bytes 5013504 | tf_op jit(solution)/shard_map/all_gather | solution.py:123
  13.2 305.5 %all-gather.20.cloned.1.call-start = ((), (), s32[]{:S(2)}) async-start(), calls=%async_computation.15 | async-start | bytes 5013504 | tf_op jit(solution)/shard_map/all_gather | solution.py:123
  13.8 537.8 %all-reduce.9.cloned.1.call-start = ((), (), s32[]{:S(2)}) async-start(), calls=%async_computation.20 | async-start | bytes 18874368
  80.6 1.5 copy-start.27
  80.6 1.6 copy-start.3
  85.4 16.3 %copy-start.13 = (bf16[1,128,768]{1,2,0:T(8,128)(2,1)}, bf16[1,128,768]{1,2,0:T(8,128)(2,1)S(1)}, u32[]{:S(2)}) copy-start(bf16[1,128,768]{1,2,0:T(8,128)(2,1)S(1)} %copy.82) | copy-start | bytes 589828
  85.6 17.2 %copy-start.14 = (bf16[1,128,768]{1,2,0:T(8,128)(2,1)}, bf16[1,128,768]{1,2,0:T(8,128)(2,1)S(1)}, u32[]{:S(2)}) copy-start(bf16[1,128,768]{1,2,0:T(8,128)(2,1)S(1)} %copy.81) | copy-start | bytes 589828
  85.7 72.2 %copy-start.20 = (bf16[1,128,768]{1,2,0:T(8,128)(2,1)}, bf16[1,128,768]{1,2,0:T(8,128)(2,1)S(1)}, u32[]{:S(2)}) copy-start(bf16[1,128,768]{1,2,0:T(8,128)(2,1)S(1)} %copy.80) | copy-start | bytes 589828
  86.5 16.5 %copy-start.18 = (bf16[12,64,128]{2,1,0:T(8,128)(2,1)}, bf16[12,64,128]{2,1,0:T(8,128)(2,1)S(1)}, u32[]{:S(2)}) copy-start(bf16[12,64,128]{2,1,0:T(8,128)(2,1)S(1)} %convolution_convert_fusion.5) | copy-start | bytes 589828
  102.5 110.1 %copy-start.5 = (bf16[128,768]{1,0:T(8,128)(2,1)}, bf16[128,768]{1,0:T(8,128)(2,1)S(1)}, u32[]{:S(2)}) copy-start(bf16[128,768]{1,0:T(8,128)(2,1)S(1)} %multiply_convert_fusion.2) | copy-start | bytes 589828
  103.0 109.6 %copy-start.7 = (bf16[160,768]{1,0:T(8,128)(2,1)}, bf16[160,768]{1,0:T(8,128)(2,1)S(1)}, u32[]{:S(2)}) copy-start(bf16[160,768]{1,0:T(8,128)(2,1)S(1)} %convolution_convert_fusion.2) | copy-start | bytes 737284
  318.7 3.4 copy-start.17
  323.7 7.0 copy-start.4
  326.5 5.8 copy-start.15
  326.5 5.8 slice-start
  326.5 7.4 slice-start.2
  330.7 3.3 copy-start.9
  330.7 1.7 slice-start.1
  330.7 3.3 slice-start.3
  332.4 3.2 copy-start.11
  348.8 1.5 copy-start
  352.6 4.4 copy-start.21
  352.8 4.3 copy-start.23
  352.9 4.1 copy-start.25
  368.0 0.9 copy-start.8
  368.0 1.2 copy-start.12
  368.1 299.6 %reduce-scatter.14.cloned.1.call-start = ((), (), s32[]{:S(2)}) async-start(), calls=%async_computation.10 | async-start | bytes 10027008 | tf_op jit(solution)/shard_map/reduce_scatter | solution.py:157
  374.9 1.0 copy-start.10
  374.9 408.0 %reduce-scatter.16.cloned.1.call-start = ((), (), s32[]{:S(2)}) async-start(), calls=%async_computation.11 | async-start | bytes 10027008 | tf_op jit(solution)/shard_map/reduce_scatter | solution.py:157
  381.0 0.9 copy-start.16
  381.0 517.5 %reduce-scatter.18.cloned.1.call-start = ((), (), s32[]{:S(2)}) async-start(), calls=%async_computation.12 | async-start | bytes 10027008 | tf_op jit(solution)/shard_map/reduce_scatter | solution.py:163
  387.0 626.8 %reduce-scatter.20.cloned.1.call-start = ((), (), s32[]{:S(2)}) async-start(), calls=%async_computation.13 | async-start | bytes 10027008 | tf_op jit(solution)/shard_map/reduce_scatter | solution.py:163
  392.1 0.9 copy-start.19
  392.1 2.8 copy-start.29
  392.1 4.1 copy-start.22
  392.1 4.1 copy-start.24
  392.1 4.1 copy-start.26
  392.1 688.5 %reduce-scatter.12.cloned.1.call-start = ((), (), s32[]{:S(2)}) async-start(), calls=%async_computation.9 | async-start | bytes 2506752 | tf_op jit(solution)/shard_map/reduce_scatter | solution.py:224
  394.8 6.0 copy-start.6
  394.8 753.0 %reduce-scatter.22.cloned.1.call-start = ((), (), s32[]{:S(2)}) async-start(), calls=%async_computation.18 | async-start | bytes 417792
  400.7 797.0 %reduce-scatter.24.cloned.1.call-start = ((), (), s32[]{:S(2)}) async-start(), calls=%async_computation.19 | async-start | bytes 417792
  401.9 679.4 %copy-start.1 = (f32[12,128,128]{1,2,0:T(8,128)S(1)}, f32[12,128,128]{1,2,0:T(8,128)}, u32[]{:S(2)}) copy-start(f32[12,128,128]{1,2,0:T(8,128)} %copy-done) | copy-start | bytes 2359300
  401.9 883.6 %all-reduce.11.cloned.1.call-start = ((), (), s32[]{:S(2)}) async-start(), calls=%async_computation.21 | async-start | bytes 6193152 | tf_op jit(solution)/shard_map/psum | solution.py:232
  1083.8 5.2 copy-start.28
  (1 other events, 0.8 us)
Sparse Core Ops, SparseCore 0:
  10.3 49.9 all-gather.13
  62.6 37.3 all-gather.15
  102.2 52.3 all-gather.21
  157.3 51.9 all-gather.17
  212.0 51.9 all-gather.23
  266.7 51.9 all-gather.19
  368.2 183.3 all-reduce.8
  556.2 111.3 reduce-scatter.13
  671.8 111.0 reduce-scatter.15
  787.4 111.1 reduce-scatter.17
  902.7 111.0 reduce-scatter.19
  1017.9 62.7 reduce-scatter.11
  1084.7 54.5 reduce-scatter.21
  1143.1 54.5 reduce-scatter.23
  1201.2 84.2 all-reduce.10
where the time goes:
time: 1300 us
  waiting for transfers between devices  1020 us (78%)
  blocking collectives  123 us (9%)
  matrix products  72.4 us (6%)
  local copies, waits for them, and re-layouts  51.6 us (4%)
  between operations  16 us (1%)
  other arithmetic  13.3 us (1%)
    reduce_scatter x2, waiting for transfers between devices, shards(): lax.psum_scatter(jnp.einsum('cd,cf->df', batch, before_grad, preferred_el...  229 us
    reduce_scatter x2, waiting for transfers between devices, shards(): lax.psum_scatter(jnp.einsum('cf,cd->fd', active, out_grad, preferred_elem...  229 us
    unnamed x18, waiting for transfers between devices  201 us
    all_gather x2, waiting for transfers between devices, shards(): whole_in = lax.all_gather(expert_in[expert], 'shard', axis=0, tiled=True)  103 us
    all_gather x2, waiting for transfers between devices, shards(): whole_out = lax.all_gather(expert_out[expert], 'shard', axis=0, tiled=True)  102 us
    psum x1, waiting for transfers between devices, shards(): lax.psum((in_shard, out_shard, gains_shard, router_shard, table_shard, ex...  81.5 us
    reduce_scatter x1, waiting for transfers between devices, shards(): lax.psum_scatter(attn_out_grad, 'shard', scatter_dimension=0, tiled=True)  64.5 us
    unnamed x1, blocking collectives  57.6 us
  transfers between devices with their start and end apart: 15, of which 13 were waited for; matrix products, arithmetic and copies ran while one was open for 6% of the time, Pallas kernels for 0%

commit v1 on v0

--- a/solution.py
+++ b/solution.py
@@ -2,10 +2,37 @@
 import jax.numpy as jnp
 from jax import lax
 from jax.sharding import PartitionSpec as P
+from jax.lax import axis_index, axis_size, ppermute
 
 BUCKETS = 32
 CAP = 80
 epsilon = 1e-06
+
+
+def point_stops_all(patch, row_dim):
+    patch = jnp.moveaxis(patch, 0, row_dim)
+    side_arr = patch.shape
+    return patch.reshape(
+        *side_arr[:row_dim], side_arr[row_dim] * side_arr[row_dim + 1], *side_arr[row_dim + 2 :]
+    )
+
+
+def _search_classes(payload, mesh_name):
+    r1 = payload[None]
+    wide_n = axis_size(mesh_name)
+    for k in range(wide_n.bit_length() - 1):
+        z2 = 1 << k
+        local_out = ppermute(r1, mesh_name, [(idx, idx ^ z2) for idx in range(wide_n)])
+        low = jnp.stack([r1, local_out], axis=0)
+        next_value = axis_index(mesh_name)
+        o_now = next_value >> k & 1
+        r1 = jnp.where(o_now == 0, low, low[::-1]).reshape(-1, *payload.shape)
+    return r1
+
+
+def pairs_all_measure(obj, field, axis_k):
+    r_now = _search_classes(obj, field)
+    return point_stops_all(r_now, axis_k)
 
 
 def rms_norm(values, gain):
@@ -117,7 +144,7 @@
     returned_list = []
     for expert in range(experts):
         batch = buffers[expert]
-        whole_in = lax.all_gather(expert_in[expert], "shard", axis=0, tiled=True)
+        whole_in = pairs_all_measure(expert_in[expert], "shard", 0)
         before = jnp.dot(batch, whole_in, preferred_element_type=jnp.float32)
         active = gelu_tanh(before).astype(jnp.bfloat16)
         whole_out = lax.all_gather(expert_out[expert], "shard", axis=0, tiled=True)

time: 1300 us -> 1480 us (1.14)
  blocking collectives: 123 us -> 207 us
  waiting for transfers between devices: 1020 us -> 1080 us
  other arithmetic: 13.3 us -> 28.7 us
    ppermute x0 -> x8, waiting for transfers between devices: none -> 158 us  [_search_classes(): ppermute(r1, mesh_name, [(idx, idx ^ z2) for idx in range(wide_n)])]
    all_gather x2, waiting for transfers between devices: 102 us -> 27.6 us  [shards(): whole_out = lax.all_gather(expert_out[expert], 'shard', axis=0, tiled=True)]
    all_gather x1, blocking collectives: 17.5 us -> 72.9 us  [shards(): lax.all_gather(router, 'shard', axis=0, tiled=True)]
    all_gather x1, blocking collectives: 23.2 us -> 53.4 us  [shards(): lax.all_gather(gains, 'shard', axis=1, tiled=True)]
    all_gather x2, waiting for transfers between devices: 103 us -> 87.1 us  [shards(): in_matrix = lax.all_gather(expert_in[expert], 'shard', axis=0, tiled=True)]
  transfers between devices with their start and end apart: 15 -> 23, of which waited for: 13 -> 16; matrix products, arithmetic and copies ran while one was open for 6% -> 8% of each run, Pallas kernels for 0% -> 0%
where the time goes in v1:
time: 1480 us; the launch traced here: 1470 us
  waiting for transfers between devices  1080 us (73%)
  blocking collectives  207 us (14%)
  matrix products  76.9 us (5%)
  local copies, waits for them, and re-layouts  61.3 us (4%)
  other arithmetic  28.7 us (2%)
  between operations  16.3 us (1%)
    reduce_scatter x2, waiting for transfers between devices, shards(): lax.psum_scatter(jnp.einsum('cd,cf->df', batch, before_grad, preferred_el...  229 us
    reduce_scatter x2, waiting for transfers between devices, shards(): lax.psum_scatter(jnp.einsum('cf,cd->fd', active, out_grad, preferred_elem...  229 us
    unnamed x18, waiting for transfers between devices  201 us
    ppermute x8, waiting for transfers between devices, _search_classes(): ppermute(r1, mesh_name, [(idx, idx ^ z2) for idx in range(wide_n)])  158 us
    all_gather x2, waiting for transfers between devices, shards(): in_matrix = lax.all_gather(expert_in[expert], 'shard', axis=0, tiled=True)  87.1 us
    psum x1, waiting for transfers between devices, shards(): lax.psum((in_shard, out_shard, gains_shard, router_shard, table_shard, ex...  81.5 us
    all_gather x1, blocking collectives, shards(): lax.all_gather(router, 'shard', axis=0, tiled=True)  72.9 us
    reduce_scatter x1, waiting for transfers between devices, shards(): lax.psum_scatter(attn_out_grad, 'shard', scatter_dimension=0, tiled=True)  64.5 us
  transfers between devices with their start and end apart: 23, of which 16 were waited for; matrix products, arithmetic and copies ran while one was open for 8% of the time, Pallas kernels for 0%

profile of v1, /device:TPU:0, one launch (start us, length us, event | category | flops | bytes accessed | tf_op | source)
XLA Modules:
  0.0 1474.1 jit_solution(1930658653076004595)
XLA Ops:
  14.3 3.0 collective-permute-start.1
  17.6 16.2 %collective-permute-done.1 = bf16[2,48,3072]{2,1,0:T(8,128)(2,1)S(1)} collective-permute-done((bf16[2,48,3072]{2,1,0:T(8,128)(2,1)S(1)}, bf16[2,48,3072]{2,1,0:T(8,128)(2,1)S(1)}, u32[]{:S(2)}, u32[]{:S(2)}) %collective-permute-start.1) | collective-permute-done | bytes 589856 | tf_op jit(solution)/shard_map/ppermute | solution.py:25
  34.1 2.2 collective-permute-start.2
  36.4 53.4 %all-gather.4 = bf16[16,48,2]{1,2,0:T(2,128)(2,1)S(1)} all-gather(bf16[1,48,2]{1,2,0:T(2,128)(2,1)S(1)} %bitcast.189), channel_id=1, replica_groups=mesh['rep'=2,'shard'=16] {'shard'}, dimensions={0}, use_global_device_ids=true | all-gather | bytes 3264 | tf_op jit(solution)/shard_map/all_gather | solution.py:90
  89.9 17.6 %all-gather.5 = bf16[16,2,12]{2,1,0:T(2,128)(2,1)S(1)} all-gather(bf16[1,2,12]{2,1,0:T(2,128)(2,1)S(1)} %bitcast.190), channel_id=1, replica_groups=mesh['rep'=2,'shard'=16] {'shard'}, dimensions={0}, use_global_device_ids=true | all-gather | bytes 816 | tf_op jit(solution)/shard_map/all_gather | solution.py:92
  110.0 59.6 %collective-permute-done.6 = bf16[4,48,3072]{2,1,0:T(8,128)(2,1)S(1)} collective-permute-done((bf16[4,48,3072]{2,1,0:T(8,128)(2,1)S(1)}, bf16[4,48,3072]{2,1,0:T(8,128)(2,1)S(1)}, u32[]{:S(2)}, u32[]{:S(2)}) %collective-permute-start.6) | collective-permute-done | bytes 1179680 | tf_op jit(solution)/shard_map/ppermute | solution.py:25
  173.6 3.9 reshape.190
  181.1 6.8 rev.37
  188.4 72.9 %all-gather.6 = bf16[16,48,2]{1,2,0:T(2,128)(2,1)S(1)} all-gather(bf16[1,48,2]{1,2,0:T(2,128)(2,1)S(1)} %bitcast.191), channel_id=1, replica_groups=mesh['rep'=2,'shard'=16] {'shard'}, dimensions={0}, use_global_device_ids=true | all-gather | bytes 3264 | tf_op jit(solution)/shard_map/all_gather | solution.py:91
  261.8 32.8 %collective-permute-done.3 = bf16[8,48,3072]{2,1,0:T(8,128)(2,1)} collective-permute-done((bf16[8,48,3072]{2,1,0:T(8,128)(2,1)S(1)}, bf16[8,48,3072]{2,1,0:T(8,128)(2,1)}, u32[]{:S(2)}, u32[]{:S(2)}) %collective-permute-start.3) | collective-permute-done | bytes 2359328 | tf_op jit(solution)/shard_map/ppermute | solution.py:25
  296.8 47.9 %collective-permute-done.7 = bf16[8,48,3072]{2,1,0:T(8,128)(2,1)} collective-permute-done((bf16[8,48,3072]{2,1,0:T(8,128)(2,1)}, bf16[8,48,3072]{2,1,0:T(8,128)(2,1)}, u32[]{:S(2)}, u32[]{:S(2)}) %collective-permute-start.7) | collective-permute-done | bytes 2359328 | tf_op jit(solution)/shard_map/ppermute | solution.py:25
  344.6 2.8 pad_maximum_fusion.1
  347.4 3.4 reverse_select_fusion.1
  350.8 3.4 reverse_select_fusion
  354.2 2.8 fusion.14
  360.9 3.4 fusion.70
  364.3 3.3 fusion.66
  367.6 4.0 fusion.10
  371.7 27.5 %all-gather.20.cloned.1.call-done = bf16[1,3072,768]{2,1,0:T(8,128)(2,1)} async-done(((bf16[1,192,768]{2,1,0:T(8,128)(2,1)}), bf16[1,3072,768]{2,1,0:T(8,128)(2,1)}) %all-gather.20.cloned.1.call-update) | async-done | bytes 4718608 | tf_op jit(solution)/shard_map/all_gather | solution.py:150
  399.2 3.4 fusion.6
  407.4 4.1 fusion.23
  411.5 41.8 %all-gather.22.cloned.1.call-done = bf16[1,768,3072]{2,1,0:T(8,128)(2,1)} async-done(((bf16[1,48,3072]{2,1,0:T(8,128)(2,1)}), bf16[1,768,3072]{2,1,0:T(8,128)(2,1)}) %all-gather.22.cloned.1.call-update) | async-done | bytes 4718608 | tf_op jit(solution)/shard_map/all_gather | solution.py:179
  453.3 4.6 fusion.2
  458.0 4.1 fusion.30
  462.1 45.3 %all-gather.24.cloned.1.call-done = bf16[1,768,3072]{2,1,0:T(8,128)(2,1)} async-done(((bf16[1,48,3072]{2,1,0:T(8,128)(2,1)}), bf16[1,768,3072]{2,1,0:T(8,128)(2,1)}) %all-gather.24.cloned.1.call-update) | async-done | bytes 4718608 | tf_op jit(solution)/shard_map/all_gather | solution.py:179
  507.4 3.9 fusion
  514.7 2.1 convert_add_fusion
  527.8 4.0 convolution_bitcast_fusion
  531.9 11.0 copy.104
  544.1 5.7 fusion.68
  550.8 5.1 fusion.64
  556.8 5.1 fusion.61
  562.0 5.0 fusion.58
  571.3 3.5 fusion.44
  577.2 149.3 %all-reduce.9.cloned.1.call-done = f32[3,768,768]{2,0,1:T(4,128)} async-done(((f32[3,768,768]{2,0,1:T(4,128)}), f32[3,768,768]{2,0,1:T(4,128)}) %all-reduce.9.cloned.1.call-update) | async-done | bytes 7077904
  728.4 114.1 %reduce-scatter.14.cloned.1.call-done = f32[48,3072]{1,0:T(8,128)} async-done(((f32[768,3072]{1,0:T(8,128)}), f32[48,3072]{1,0:T(8,128)}) %reduce-scatter.14.cloned.1.call-update) | async-done | bytes 589840 | tf_op jit(solution)/shard_map/reduce_scatter | solution.py:184
  842.5 115.2 %reduce-scatter.16.cloned.1.call-done = f32[48,3072]{1,0:T(8,128)} async-done(((f32[768,3072]{1,0:T(8,128)}), f32[48,3072]{1,0:T(8,128)}) %reduce-scatter.16.cloned.1.call-update) | async-done | bytes 589840 | tf_op jit(solution)/shard_map/reduce_scatter | solution.py:184
  957.8 2.3 pad_maximum_fusion.6
  960.1 113.3 %reduce-scatter.18.cloned.1.call-done = f32[192,768]{1,0:T(8,128)} async-done(((f32[3072,768]{1,0:T(8,128)}), f32[192,768]{1,0:T(8,128)}) %reduce-scatter.18.cloned.1.call-update) | async-done | bytes 589840 | tf_op jit(solution)/shard_map/reduce_scatter | solution.py:190
  1073.4 115.2 %reduce-scatter.20.cloned.1.call-done = f32[192,768]{1,0:T(8,128)} async-done(((f32[3072,768]{1,0:T(8,128)}), f32[192,768]{1,0:T(8,128)}) %reduce-scatter.20.cloned.1.call-update) | async-done | bytes 589840 | tf_op jit(solution)/shard_map/reduce_scatter | solution.py:190
  1188.7 2.4 pad_maximum_fusion.7
  1191.1 64.5 %reduce-scatter.12.cloned.1.call-done = f32[48,768]{1,0:T(8,128)} async-done(((f32[768,768]{1,0:T(8,128)}), f32[48,768]{1,0:T(8,128)}) %reduce-scatter.12.cloned.1.call-update) | async-done | bytes 147472 | tf_op jit(solution)/shard_map/reduce_scatter | solution.py:251
  1258.5 3.4 reshape.203
  1263.9 57.6 %all-reduce.3 = f32[32,12]{1,0:T(8,128)S(1)} all-reduce(f32[32,12]{1,0:T(8,128)S(1)} %fusion.77), channel_id=10, replica_groups=mesh['rep'=2,'shard'=16] {'shard'}, use_global_device_ids=true, to_apply=%region_27.29.clone | all-reduce | flops 384 | bytes 3072
  1323.3 49.3 %reduce-scatter.24.cloned.1.call-done = f32[48,2]{1,0:T(8,128)} async-done(((f32[768,2]{1,0:T(8,128)}), f32[48,2]{1,0:T(8,128)}) %reduce-scatter.24.cloned.1.call-update) | async-done | bytes 400
  1373.4 5.5 all-reduce.4
  1378.9 81.5 %all-reduce.11.cloned.1.call-done = (f32[3,48,768]{2,0,1:T(4,128)}, f32[48,768]{1,0:T(8,128)}, f32[2,48,3072]{2,1,0:T(8,128)}, f32[2,192,768]{2,1,0:T(8,128)}) async-done(((f32[3,48,768]{2,0,1:T(4,128)}, f32[48,768]{1,0:T(8,128)}, f32[2,48,3072]{2,1,0:T(8,128)}, f32[2,192,768]{2,1,0:T(8,128)}), (f32[3,48,768]{2,0,1:T(4,128)}, f32[48,768]{1,0:T(8,128)}, f32[2,48,3072]{2,1,0:T(8,128)}, ...) | async-done | bytes 2949136 | tf_op jit(solution)/shard_map/psum | solution.py:259
  1464.0 2.4 copy.126
  (229 shorter events, 66.1 us)
Async XLA Ops:
  7.2 4.1 copy-start.35
  7.2 347.1 %all-gather.14.cloned.1.call-start = ((), (), s32[]{:S(2)}) async-start(), calls=%async_computation.7 | async-start | bytes 3760128 | tf_op jit(solution)/shard_map/all_gather | solution.py:88
  7.9 350.5 %all-gather.16.cloned.1.call-start = ((), (), s32[]{:S(2)}) async-start(), calls=%async_computation.8 | async-start | bytes 1253376 | tf_op jit(solution)/shard_map/all_gather | solution.py:89
  8.7 359.0 %all-gather.18.cloned.1.call-start = ((), (), s32[]{:S(2)}) async-start(), calls=%async_computation.14 | async-start | bytes 5013504 | tf_op jit(solution)/shard_map/all_gather | solution.py:150
  10.6 388.6 %all-gather.20.cloned.1.call-start = ((), (), s32[]{:S(2)}) async-start(), calls=%async_computation.15 | async-start | bytes 5013504 | tf_op jit(solution)/shard_map/all_gather | solution.py:150
  11.2 442.1 %all-gather.22.cloned.1.call-start = ((), (), s32[]{:S(2)}) async-start(), calls=%async_computation.16 | async-start | bytes 5013504 | tf_op jit(solution)/shard_map/all_gather | solution.py:179
  12.1 5.4 copy-start.19
  12.2 495.3 %all-gather.24.cloned.1.call-start = ((), (), s32[]{:S(2)}) async-start(), calls=%async_computation.17 | async-start | bytes 5013504 | tf_op jit(solution)/shard_map/all_gather | solution.py:179
  12.2 1.9 collective-permute-start
  12.7 4.5 collective-permute-start.4
  14.3 19.4 %collective-permute-start.1 = (bf16[2,48,3072]{2,1,0:T(8,128)(2,1)S(1)}, bf16[2,48,3072]{2,1,0:T(8,128)(2,1)S(1)}, u32[]{:S(2)}, u32[]{:S(2)}) collective-permute-start(bf16[2,48,3072]{2,1,0:T(8,128)(2,1)S(1)} %get-tuple-element.65), channel_id=1, source_target_pairs={{0,2},{1,3},{2,0},{3,1},{4,6},{5,7},{6,4},{7,5},{8,10},{9,11},{10,... | collective-permute-start | bytes 1769480 | tf_op jit(solution)/shard_map/ppermute | solution.py:25
  17.5 90.0 %collective-permute-start.5 = (bf16[2,48,3072]{2,1,0:T(8,128)(2,1)S(1)}, bf16[2,48,3072]{2,1,0:T(8,128)(2,1)}, u32[]{:S(2)}, u32[]{:S(2)}) collective-permute-start(bf16[2,48,3072]{2,1,0:T(8,128)(2,1)S(1)} %get-tuple-element.73), channel_id=1, source_target_pairs={{0,2},{1,3},{2,0},{3,1},{4,6},{5,7},{6,4},{7,5},{8,10},{9,11},{10,... | collective-permute-start | bytes 1769480 | tf_op jit(solution)/shard_map/ppermute | solution.py:25
  33.8 56.1 %copy-start.38 = (bf16[2,12]{1,0:T(2,128)(2,1)S(1)}, bf16[2,12]{1,0:T(2,128)(2,1)}, u32[]{:S(2)}) copy-start(bf16[2,12]{1,0:T(2,128)(2,1)} %param.23) | copy-start | bytes 148
  34.1 74.9 %collective-permute-start.2 = (bf16[4,48,3072]{2,1,0:T(8,128)(2,1)S(1)}, bf16[4,48,3072]{2,1,0:T(8,128)(2,1)S(1)}, u32[]{:S(2)}, u32[]{:S(2)}) collective-permute-start(bf16[4,48,3072]{2,1,0:T(8,128)(2,1)S(1)} %bitcast.151), channel_id=1, source_target_pairs={{0,4},{1,5},{2,6},{3,7},{4,0},{5,1},{6,2},{7,3},{8,12},{9,13},{10,... | collective-permute-start | bytes 3538952 | tf_op jit(solution)/shard_map/ppermute | solution.py:25
  36.3 690.1 %all-reduce.9.cloned.1.call-start = ((), (), s32[]{:S(2)}) async-start(), calls=%async_computation.20 | async-start | bytes 18874368
  109.0 60.6 %collective-permute-start.6 = (bf16[4,48,3072]{2,1,0:T(8,128)(2,1)S(1)}, bf16[4,48,3072]{2,1,0:T(8,128)(2,1)S(1)}, u32[]{:S(2)}, u32[]{:S(2)}) collective-permute-start(bf16[4,48,3072]{2,1,0:T(8,128)(2,1)S(1)} %bitcast.153), channel_id=1, source_target_pairs={{0,4},{1,5},{2,6},{3,7},{4,0},{5,1},{6,2},{7,3},{8,12},{9,13},{10,... | collective-permute-start | bytes 3538952 | tf_op jit(solution)/shard_map/ppermute | solution.py:25
  109.9 184.8 %collective-permute-start.3 = (bf16[8,48,3072]{2,1,0:T(8,128)(2,1)S(1)}, bf16[8,48,3072]{2,1,0:T(8,128)(2,1)}, u32[]{:S(2)}, u32[]{:S(2)}) collective-permute-start(bf16[8,48,3072]{2,1,0:T(8,128)(2,1)S(1)} %bitcast.146), channel_id=1, source_target_pairs={{0,8},{1,9},{2,10},{3,11},{4,12},{5,13},{6,14},{7,15},{8,0},{9,1},... | collective-permute-start | bytes 7077896 | tf_op jit(solution)/shard_map/ppermute | solution.py:25
  171.8 172.8 %collective-permute-start.7 = (bf16[8,48,3072]{2,1,0:T(8,128)(2,1)}, bf16[8,48,3072]{2,1,0:T(8,128)(2,1)}, u32[]{:S(2)}, u32[]{:S(2)}) collective-permute-start(bf16[8,48,3072]{2,1,0:T(8,128)(2,1)} %bitcast.41), channel_id=1, source_target_pairs={{0,8},{1,9},{2,10},{3,11},{4,12},{5,13},{6,14},{7,15},{8,0},{9,1},... | collective-permute-start | bytes 7077896 | tf_op jit(solution)/shard_map/ppermute | solution.py:25
  179.8 8.1 copy-start.41
  179.8 8.2 copy-start.36
  179.8 8.6 copy-start.39
  179.8 81.8 %copy-start.3 = (bf16[128,768]{1,0:T(8,128)(2,1)S(1)}, bf16[128,768]{1,0:T(8,128)(2,1)}, u32[]{:S(2)}) copy-start(bf16[128,768]{1,0:T(8,128)(2,1)} %param.14) | copy-start | bytes 589828
  358.4 5.9 copy-start.26
  360.3 4.0 copy-start.6
  360.9 3.4 copy-start.8
  399.2 3.4 copy-start.24
  411.5 41.8 %copy-start.12 = (bf16[80,3072]{1,0:T(8,128)(2,1)}, bf16[80,3072]{1,0:T(8,128)(2,1)S(1)}, u32[]{:S(2)}) copy-start(bf16[80,3072]{1,0:T(8,128)(2,1)S(1)} %fusion.23) | copy-start | bytes 1474564
  453.3 4.6 copy-start.22
  462.1 45.4 %copy-start.10 = (bf16[80,3072]{1,0:T(8,128)(2,1)}, bf16[80,3072]{1,0:T(8,128)(2,1)S(1)}, u32[]{:S(2)}) copy-start(bf16[80,3072]{1,0:T(8,128)(2,1)S(1)} %fusion.30) | copy-start | bytes 1474564
  507.4 3.9 copy-start.25
  513.0 3.9 copy-start.4
  525.5 6.3 copy-start.29
  526.7 5.2 copy-start.31
  527.8 4.0 copy-start.33
  542.9 299.6 %reduce-scatter.14.cloned.1.call-start = ((), (), s32[]{:S(2)}) async-start(), calls=%async_computation.10 | async-start | bytes 10027008 | tf_op jit(solution)/shard_map/reduce_scatter | solution.py:184
  549.8 408.0 %reduce-scatter.16.cloned.1.call-start = ((), (), s32[]{:S(2)}) async-start(), calls=%async_computation.11 | async-start | bytes 10027008 | tf_op jit(solution)/shard_map/reduce_scatter | solution.py:184
  555.9 517.5 %reduce-scatter.18.cloned.1.call-start = ((), (), s32[]{:S(2)}) async-start(), calls=%async_computation.12 | async-start | bytes 10027008 | tf_op jit(solution)/shard_map/reduce_scatter | solution.py:190
  561.9 626.7 %reduce-scatter.20.cloned.1.call-start = ((), (), s32[]{:S(2)}) async-start(), calls=%async_computation.13 | async-start | bytes 10027008 | tf_op jit(solution)/shard_map/reduce_scatter | solution.py:190
  567.0 4.3 copy-start.30
  567.0 4.3 copy-start.32
  567.1 4.3 copy-start.34
  567.1 688.5 %reduce-scatter.12.cloned.1.call-start = ((), (), s32[]{:S(2)}) async-start(), calls=%async_computation.9 | async-start | bytes 2506752 | tf_op jit(solution)/shard_map/reduce_scatter | solution.py:251
  569.8 752.7 %reduce-scatter.22.cloned.1.call-start = ((), (), s32[]{:S(2)}) async-start(), calls=%async_computation.18 | async-start | bytes 417792
  571.3 4.6 copy-start.7
  575.9 796.7 %reduce-scatter.24.cloned.1.call-start = ((), (), s32[]{:S(2)}) async-start(), calls=%async_computation.19 | async-start | bytes 417792
  577.1 883.3 %all-reduce.11.cloned.1.call-start = ((), (), s32[]{:S(2)}) async-start(), calls=%async_computation.21 | async-start | bytes 6193152 | tf_op jit(solution)/shard_map/psum | solution.py:259
  1188.7 67.5 %copy-start.1 = (f32[12,128,128]{1,2,0:T(8,128)S(1)}, f32[12,128,128]{1,2,0:T(8,128)}, u32[]{:S(2)}) copy-start(f32[12,128,128]{1,2,0:T(8,128)} %copy-done) | copy-start | bytes 2359300
  1460.4 6.0 copy-start.20
  (18 other events, 29.8 us)
Sparse Core Ops, SparseCore 0:
  10.3 59.5 all-gather.13
  72.2 42.5 all-gather.15
  117.6 169.1 all-gather.17
  289.0 110.1 all-gather.19
  401.3 51.9 all-gather.21
  455.4 51.9 all-gather.23
  543.0 183.3 all-reduce.8
  731.1 111.3 reduce-scatter.13
  846.6 111.0 reduce-scatter.15
  962.3 111.1 reduce-scatter.17
  1077.5 111.0 reduce-scatter.19
  1192.8 62.7 reduce-scatter.11
  1259.6 54.5 reduce-scatter.21
  1318.0 54.5 reduce-scatter.23
  1376.1 84.2 all-reduce.10
